TPU v7x, 32 devices: a whole 2x2x4 slice. The times are simulated.
32 devices in a mesh: group: 2 (over x), gx: 16 (over z, y, core).
Axes of the slice: x: 2, y: 2, z: 4, core: 2. Of those that a mesh axis runs over, the one named last changes fastest.
Arguments:
- hidden: bfloat16 [2, 64, 16384], P(None, ('group', 'gx')), parts along dimension 1, may hold values from -6 to 6
- norm_gain: bfloat16 [16384], replicated, may hold values from 0.5 to 1.5
- w_query: bfloat16 [16384, 8192], P(None, 'gx'), may hold values from -0.046875 to 0.046875
- w_keyval: bfloat16 [2, 16384, 512], P(None, 'gx'), may hold values from -0.046875 to 0.046875
- w_out: bfloat16 [8192, 16384], P(None, 'gx'), may hold values from -0.5 to 0.5
- kv_cache: bfloat16 [2, 64, 1024, 512], P(None, ('group', 'gx')), parts along dimension 1, may hold values from -1700 to 1700
- lengths: int32 [64], P(('group', 'gx')), parts along dimension 0, may hold values from 1 to 1024, as said below
Outputs:
- attended: bfloat16 [2, 64, 16384], P(None, ('group', 'gx')), parts along dimension 1
There are 2 independent parts, one for each index of `group`. A program takes and returns all parts, laid end to end along the dimension named above; an argument that names none is the same for every part. Nothing has to cross between parts.
Inputs may be any that keep to these rules, and one draw needn't show every extreme that they name: `lengths`: some row has exactly 1024 valid entries in every draw.
All inputs are finite; a program needn't handle non-finite values.
Results may differ from a plain program's by a relative error of at most 0.0055.
The roundings to bfloat16 on the way count: a program that leaves them out, or rounds other values in their place, can miss the bound.
Values may be sent and summed in bfloat16 or wider, within the bound.
No kernel may reach another device: no remote copies, remote signals or barrier semaphores. Data moves between devices by JAX's collectives and lax.ppermute only.
A program may use at most 192 MiB of HBM per device.

v0:
```python
import math

import jax
import jax.numpy as jnp
from jax import lax
from jax.sharding import PartitionSpec as P

HD = 128


ROPE_BASE = 500000.0
EPSILON = 1e-05


def rotate(values, positions):
    row_total, head_count, head_width = values.shape
    half_width = head_width // 2
    frequency = ROPE_BASE ** (-2.0 * jnp.arange(half_width, dtype=jnp.float32) / head_width)
    angles = positions[:, None, None] * frequency[None, None, :]
    cosine = jnp.cos(angles)
    sine_part = jnp.sin(angles)
    paired = values.reshape(row_total, head_count, half_width, 2)
    first_half = paired[..., 0]
    second_half = paired[..., 1]
    turned = jnp.stack(
        [
            first_half * cosine - second_half * sine_part,
            first_half * sine_part + second_half * cosine,
        ],
        -1,
    )
    return turned.reshape(row_total, head_count, head_width)


def attend(queries, cache_keys, cache_values, lengths, fresh_keys, fresh_values):
    score_scale = 1.0 / math.sqrt(HD)
    fresh_scores = (
        jnp.einsum("rkgd,rskd->rkgs", queries, fresh_keys, preferred_element_type=jnp.float32)
        * score_scale
    )
    cached = (
        jnp.einsum("rkgd,rlkd->rkgl", queries, cache_keys, preferred_element_type=jnp.float32)
        * score_scale
    )
    in_range = jnp.arange(cache_keys.shape[1])[None, :] < lengths[:, None]
    cached = jnp.where(in_range[:, None, None, :], cached, -jnp.inf)
    row_peak = jnp.maximum(cached.max(-1), fresh_scores.max(-1))
    cached_exp = jnp.exp(cached - row_peak[..., None])
    fresh_exp = jnp.exp(fresh_scores - row_peak[..., None])
    denominator = cached_exp.sum(-1) + fresh_exp.sum(-1)
    mixed = jnp.einsum(
        "rkgl,rlkd->rkgd",
        cached_exp.astype(jnp.bfloat16),
        cache_values,
        preferred_element_type=jnp.float32,
    )
    mixed = mixed + jnp.einsum(
        "rkgs,rskd->rkgd",
        fresh_exp.astype(jnp.bfloat16),
        fresh_values,
        preferred_element_type=jnp.float32,
    )
    return (mixed / denominator[..., None]).astype(jnp.bfloat16)


def body(hidden, norm_gain, w_query, w_keyval, w_out, kv_cache, lengths):
    step_count, rows_dev, model_width = hidden.shape
    devices = lax.axis_size("gx")
    device_index = lax.axis_index("gx")
    row_slab = w_keyval.shape[1]
    kv_width = w_keyval.shape[2]
    query_cols = w_query.shape[1]
    heads_width = query_cols * devices
    head_count = heads_width // HD
    kv_heads = kv_width // HD
    kv_both = jnp.concatenate([w_keyval[0], w_keyval[1]], 1)
    cache_keys = kv_cache[0].reshape(rows_dev, kv_cache.shape[2], kv_heads, HD)
    cache_values = kv_cache[1].reshape(rows_dev, kv_cache.shape[2], kv_heads, HD)
    states = hidden.astype(jnp.float32)
    scaled = states * lax.rsqrt(jnp.mean(states * states, -1, keepdims=True) + EPSILON)
    normed = (scaled * norm_gain.astype(jnp.float32)).astype(jnp.bfloat16)
    new_keys = []
    new_values = []
    outputs = []
    for step_index in range(step_count):
        shard_piece = lax.all_gather(normed[step_index], "gx", axis=0, tiled=True)
        queries = jnp.dot(shard_piece, w_query, preferred_element_type=jnp.float32)
        own_slab = lax.dynamic_slice_in_dim(shard_piece, device_index * row_slab, row_slab, 1)
        partial_kv = jnp.dot(own_slab, kv_both, preferred_element_type=jnp.float32)
        joined = jnp.concatenate([queries, partial_kv], 1)
        project_query_rows = lax.all_to_all(
            joined[:, :query_cols], "gx", split_axis=0, concat_axis=1, tiled=True
        )
        project_keyval = lax.psum_scatter(
            joined[:, query_cols:], "gx", scatter_dimension=0, tiled=True
        )
        positions = (lengths + step_index).astype(jnp.float32)
        prepare_queries = rotate(
            project_query_rows.reshape(rows_dev, head_count, HD), positions
        ).astype(jnp.bfloat16)
        prepare_queries = prepare_queries.reshape(rows_dev, kv_heads, head_count // kv_heads, HD)
        key_new = rotate(
            project_keyval[:, :kv_width].reshape(rows_dev, kv_heads, HD), positions
        ).astype(jnp.bfloat16)
        value_new = (
            project_keyval[:, kv_width:].reshape(rows_dev, kv_heads, HD).astype(jnp.bfloat16)
        )
        queries, key_new, value_new = (prepare_queries, key_new, value_new)
        new_keys.append(key_new)
        new_values.append(value_new)
        mixed = attend(
            queries,
            cache_keys,
            cache_values,
            lengths,
            jnp.stack(new_keys, 1),
            jnp.stack(new_values, 1),
        )
        out_cols = jnp.dot(
            lax.all_gather(mixed.reshape(rows_dev, heads_width), "gx", axis=0, tiled=True),
            w_out,
            preferred_element_type=jnp.float32,
        ).astype(jnp.bfloat16)
        outputs.append(lax.all_to_all(out_cols, "gx", split_axis=0, concat_axis=1, tiled=True))
    return jnp.stack(outputs)


def solution(mesh):
    in_specs = (
        P(None, ("group", "gx"), None),
        P(),
        P(None, "gx"),
        P(None, "gx", None),
        P(None, "gx"),
        P(None, ("group", "gx"), None, None),
        P(("group", "gx")),
    )
    out_specs = P(None, ("group", "gx"), None)
    return jax.shard_map(body, mesh=mesh, in_specs=in_specs, out_specs=out_specs, check_vma=False)
```

profile of v0, /device:TPU:0, one launch (start us, length us, event | category | flops | bytes accessed | tf_op | source)
XLA Modules:
  0.0 313.3 jit_solution(3966684500343303501)
XLA Ops:
  11.3 3.9 %fusion.41 = (bf16[1,2,1024,512]{3,2,1,0:T(8,128)(2,1)S(1)}, bf16[1,2,1024,512]{3,2,1,0:T(8,128)(2,1)}) fusion(bf16[2,2,1024,512]{3,2,1,0:T(8,128)(2,1)} %param.12), kind=kLoop, calls=%fused_computation.99 | loop fusion | bytes 8388608 | tf_op jit(solution)/shard_map/slice | solution.py:77
  17.8 3.0 copy.122
  24.9 29.9 %all-gather.7.cloned.1.call-done = bf16[1,32,16384]{2,0,1:T(2,128)(2,1)} async-done(((bf16[1,2,16384]{2,0,1:T(2,128)(2,1)}), bf16[1,32,16384]{2,0,1:T(2,128)(2,1)}) %all-gather.7.cloned.1.call-update) | async-done | bytes 1048592 | tf_op jit(solution)/shard_map/all_gather | solution.py:86
  54.8 9.5 %fusion.11 = f32[32,512]{1,0:T(8,128)S(1)} fusion(bf16[16384,512]{1,0:T(8,128)(2,1)} %param.9, bf16[1,32,16384]{2,0,1:T(2,128)(2,1)} %all-gather.7.cloned.1.call-done), kind=kOutput, calls=%fused_computation.27 | convolution fusion | flops 536870912 | bytes 17891328 | tf_op jit(solution)/shard_map/dot_general | solution.py:87
  64.9 3.5 %all-to-all-start = ((f32[16,2,512]{2,1,0:T(2,128)}), f32[16,2,512]{2,1,0:T(2,128)S(1)}, u32[]{:S(2)}, u32[]{:S(2)}) async-start(f32[16,2,512]{2,1,0:T(2,128)} %all_to_all.48), calls=%async_computation | async-start | bytes 131072 | tf_op jit(solution)/shard_map/all_to_all | solution.py:91
  68.4 29.9 %all-gather.9.cloned.1.call-done = bf16[1,32,16384]{2,0,1:T(2,128)(2,1)} async-done(((bf16[1,2,16384]{2,0,1:T(2,128)(2,1)}), bf16[1,32,16384]{2,0,1:T(2,128)(2,1)}) %all-gather.9.cloned.1.call-update) | async-done | bytes 1048592 | tf_op jit(solution)/shard_map/all_gather | solution.py:86
  98.3 9.6 %fusion.8 = f32[32,512]{1,0:T(8,128)S(1)} fusion(bf16[16384,512]{1,0:T(8,128)(2,1)} %param.9, bf16[1,32,16384]{2,0,1:T(2,128)(2,1)} %all-gather.9.cloned.1.call-done), kind=kOutput, calls=%fused_computation.24 | convolution fusion | flops 536870912 | bytes 17891328 | tf_op jit(solution)/shard_map/dot_general | solution.py:87
  111.8 3.5 %all-to-all-start.2 = ((f32[16,2,512]{2,1,0:T(2,128)}), f32[16,2,512]{2,1,0:T(2,128)S(1)}, u32[]{:S(2)}, u32[]{:S(2)}) async-start(f32[16,2,512]{2,1,0:T(2,128)} %all_to_all.54), calls=%async_computation.2 | async-start | bytes 131072 | tf_op jit(solution)/shard_map/all_to_all | solution.py:91
  117.9 5.5 %reshape_reshape.12 = f32[2,64,64,2]{3,2,1,0:T(8,128)} reshape(f32[2,16,512]{2,1,0:T(8,128)S(1)} %copy.72) | data formatting | bytes 131072 | tf_op jit(solution)/shard_map/reshape;reshape | solution.py:22
  123.4 5.6 %reshape_reshape.14 = f32[2,64,64,2]{3,2,1,0:T(8,128)} reshape(f32[2,16,512]{2,1,0:T(8,128)S(1)} %copy.90) | data formatting | bytes 131072 | tf_op jit(solution)/shard_map/reshape;reshape | solution.py:22
  129.0 19.3 %slice_multiply_fusion.1 = (f32[2,64,64,1]{3,2,1,0:T(8,128)}, f32[2,64,64,1]{3,2,1,0:T(8,128)}, f32[2,64,64,1]{3,2,1,0:T(8,128)}, f32[2,64,64,1]{3,2,1,0:T(8,128...) fusion(f32[2,64,64,2]{3,2,1,0:T(8,128)} %reshape_reshape.14, ...), kind=kLoop, calls=%fused_computation.1 | loop fusion | flops 65536 | bytes 395264 | tf_op jit(solution)/shard_map/mul | solution.py:27
  151.2 3.0 copy.74
  154.2 3.0 copy.75
  157.2 3.0 copy.76
  160.6 3.0 copy.91
  163.6 3.0 copy.92
  169.6 3.0 copy.94
  177.2 32.6 %all-reduce.5.cloned.1.call-done = (f32[32,1024]{1,0:T(8,128)}, f32[32,1024]{1,0:T(8,128)}) async-done(((f32[32,1024]{1,0:T(8,128)}, f32[32,1024]{1,0:T(8,128)}), (f32[32,1024]{1,0:T(8,128)}, f32[32,1024]{1,0:T(8,128)})) %all-reduce.5.cloned.1.call-update) | async-done | bytes 262160
  228.3 22.5 %all-gather.2 = bf16[16,2,8192]{2,1,0:T(2,128)(2,1)S(1)} all-gather(bf16[1,2,8192]{2,1,0:T(2,128)(2,1)S(1)} %reshape.259), channel_id=1, replica_groups=mesh['group'=2,'gx'=16] {'gx'}, dimensions={0}, use_global_device_ids=true | all-gather | bytes 557056 | tf_op jit(solution)/shard_map/all_gather | solution.py:120
  251.0 8.7 %convolution_convert_fusion.1 = bf16[32,1024]{1,0:T(8,128)(2,1)S(1)} fusion(bf16[32,8192]{1,0:T(8,128)(2,1)S(1)} %reshape.260, bf16[8192,1024]{1,0:T(8,128)(2,1)} %param.11), kind=kOutput, calls=%fused_computation.16 | convolution fusion | flops 536903680 | bytes 17367040 | tf_op jit(solution)/shard_map/dot_general | solution.py:119
  260.4 3.5 %all-to-all-start.1 = ((bf16[16,2,1024]{2,1,0:T(2,128)(2,1)}), bf16[16,2,1024]{2,1,0:T(2,128)(2,1)S(1)}, u32[]{:S(2)}, u32[]{:S(2)}) async-start(bf16[16,2,1024]{2,1,0:T(2,128)(2,1)} %all_to_all.51), calls=%async_computation.1 | async-start | bytes 131072 | tf_op jit(solution)/shard_map/all_to_all | solution.py:124
  264.2 23.2 %all-gather.3 = bf16[16,2,8192]{2,1,0:T(2,128)(2,1)S(1)} all-gather(bf16[1,2,8192]{2,1,0:T(2,128)(2,1)S(1)} %reshape.261), channel_id=1, replica_groups=mesh['group'=2,'gx'=16] {'gx'}, dimensions={0}, use_global_device_ids=true | all-gather | bytes 557056 | tf_op jit(solution)/shard_map/all_gather | solution.py:120
  287.6 8.7 %convolution_convert_fusion = bf16[32,1024]{1,0:T(8,128)(2,1)S(1)} fusion(bf16[32,8192]{1,0:T(8,128)(2,1)S(1)} %reshape.262, bf16[8192,1024]{1,0:T(8,128)(2,1)} %param.11), kind=kOutput, calls=%fused_computation.15 | convolution fusion | flops 536903680 | bytes 17367040 | tf_op jit(solution)/shard_map/dot_general | solution.py:119
  296.5 9.5 %all_to_all.64 = bf16[16,2,1024]{2,1,0:T(2,128)(2,1)S(1)} all-to-all(bf16[16,2,1024]{2,1,0:T(2,128)(2,1)S(1)} %all_to_all.57), channel_id=1, replica_groups=mesh['group'=2,'gx'=16] {'gx'}, dimensions={0} | all-to-all | bytes 131072 | tf_op jit(solution)/shard_map/all_to_all | solution.py:124
  (99 shorter events, 49.3 us)
Async XLA Ops:
  6.5 48.3 %all-gather.7.cloned.1.call-start = ((), (), s32[]{:S(2)}) async-start(), calls=%async_computation.4 | async-start | bytes 2228224 | tf_op jit(solution)/shard_map/all_gather | solution.py:86
  10.6 87.8 %all-gather.9.cloned.1.call-start = ((), (), s32[]{:S(2)}) async-start(), calls=%async_computation.5 | async-start | bytes 2228224 | tf_op jit(solution)/shard_map/all_gather | solution.py:86
  15.3 5.5 %copy-start.2 = (u32[32]{0:T(128)S(1)}, u32[32]{0:T(128)}, u32[]{:S(2)}) copy-start(u32[32]{0:T(128)} %constant.39) | copy-start | bytes 388
  15.3 6.7 %copy-start.1 = (s32[2]{0:T(128)S(1)}, s32[2]{0:T(128)}, u32[]{:S(2)}) copy-start(s32[2]{0:T(128)} %param.13) | copy-start | bytes 28
  64.9 46.8 %all-to-all-start = ((f32[16,2,512]{2,1,0:T(2,128)}), f32[16,2,512]{2,1,0:T(2,128)S(1)}, u32[]{:S(2)}, u32[]{:S(2)}) async-start(f32[16,2,512]{2,1,0:T(2,128)} %all_to_all.48), calls=%async_computation | async-start | bytes 131072 | tf_op jit(solution)/shard_map/all_to_all | solution.py:91
  98.3 10.6 %copy-start = (bf16[1024,512]{1,0:T(8,128)(2,1)S(1)}, bf16[1024,512]{1,0:T(8,128)(2,1)}, u32[]{:S(2)}) copy-start(bf16[1024,512]{1,0:T(8,128)(2,1)} %get-tuple-element.22) | copy-start | bytes 3145732
  111.8 11.6 %all-to-all-start.2 = ((f32[16,2,512]{2,1,0:T(2,128)}), f32[16,2,512]{2,1,0:T(2,128)S(1)}, u32[]{:S(2)}, u32[]{:S(2)}) async-start(f32[16,2,512]{2,1,0:T(2,128)} %all_to_all.54), calls=%async_computation.2 | async-start | bytes 131072 | tf_op jit(solution)/shard_map/all_to_all | solution.py:91
  115.3 94.6 %all-reduce.5.cloned.1.call-start = ((), (), s32[]{:S(2)}) async-start(), calls=%async_computation.6 | async-start | bytes 524288
  260.4 36.0 %all-to-all-start.1 = ((bf16[16,2,1024]{2,1,0:T(2,128)(2,1)}), bf16[16,2,1024]{2,1,0:T(2,128)(2,1)S(1)}, u32[]{:S(2)}, u32[]{:S(2)}) async-start(bf16[16,2,1024]{2,1,0:T(2,128)(2,1)} %all_to_all.51), calls=%async_computation.1 | async-start | bytes 131072 | tf_op jit(solution)/shard_map/all_to_all | solution.py:124
Sparse Core Ops, SparseCore 0:
  10.7 44.0 all-gather.6
  57.0 41.3 all-gather.8
  119.5 90.2 all-reduce.4
where the time goes:
time: 315 us; the launch traced here: 313 us
  waiting for transfers between devices  93.2 us (30%)
  local copies, waits for them, and re-layouts  67.3 us (21%)
  blocking collectives  55.2 us (18%)
  matrix products  46 us (15%)
  other arithmetic  26.8 us (9%)
  between operations  14.1 us (4%)
  starting transfers between devices  10.8 us (3%)
    all_gather x2, waiting for transfers between devices, body(): shard_piece = lax.all_gather(normed[step_index], 'gx', axis=0, tiled=True)  59.8 us
    all_gather x2, blocking collectives, body(): lax.all_gather(mixed.reshape(rows_dev, heads_width), 'gx', axis=0, tiled=...  45.8 us
    unnamed x4, waiting for transfers between devices  33.3 us
    mul x2, other arithmetic, rotate(): second_half * sine_part  22 us
    dot_general x2, matrix products, body(): queries = jnp.dot(shard_piece, w_query, preferred_element_type=jnp.float32)  19 us
    dot_general x2, matrix products, body(): jnp.dot(lax.all_gather(mixed.reshape(rows_dev, heads_width), 'gx', axis=0...  17.5 us
    another operation x4, local copies, waits for them, and re-layouts, rotate(): paired = values.reshape(row_total, head_count, half_width, 2)  12.2 us
    all_to_all x1, blocking collectives, body(): lax.all_to_all(out_cols, 'gx', split_axis=0, concat_axis=1, tiled=True)  9.48 us
  transfers between devices with their start and end apart: 6, of which 3 were waited for; matrix products, arithmetic and copies ran while one was open for 34% of the time, Pallas kernels for 0%

commit v1 on v0

--- a/solution.py
+++ b/solution.py
@@ -1,15 +1,424 @@
+import functools
 import math
 
 import jax
 import jax.numpy as jnp
+import numpy as np
 from jax import lax
+from jax.experimental import pallas as pl
+from jax.experimental.pallas import tpu as pltpu
 from jax.sharding import PartitionSpec as P
 
 HD = 128
-
-
 ROPE_BASE = 500000.0
 EPSILON = 1e-05
+TAG = 128
+VMEM_LIMIT = 48 * 1024 * 1024
+VMEM = pl.BlockSpec(memory_space=pltpu.VMEM)
+SMEM = pl.BlockSpec(memory_space=pltpu.SMEM)
+HBM = pl.BlockSpec(memory_space=pltpu.HBM)
+
+
+def permute(block, target):
+    return lax.ppermute(block, "gx", [(int(i), int(t)) for i, t in enumerate(target)])
+
+
+def moved(source, target):
+    result = np.empty_like(source)
+    result[target] = source
+    return result
+
+
+class Slot:
+    def __init__(self, parts, source):
+        self.parts, self.source = parts, source
+
+    def send(self, target):
+        return Slot([permute(part, target) for part in self.parts], moved(self.source, target))
+
+
+def halves(block, middle):
+    return block[:, :middle], block[:, middle:]
+
+
+def ring_order(size):
+    if size > 4:
+        return list(range(size))
+    return list(range(0, size, 2)) + list(range(1, size, 2))[::-1]
+
+
+def axes_of(devices):
+    chips, inner = devices // 2, 1
+    while inner * inner * 4 <= chips and chips % (inner * 2) == 0:
+        inner *= 2
+    sizes = (chips // inner, inner, 2)
+    place = np.arange(devices).reshape(sizes)
+    result = []
+    for axis, size in enumerate(sizes):
+        order = ring_order(size)
+        after = np.empty(size, int)
+        for here, there in zip(order, order[1:] + order[:1]):
+            after[here] = there
+        before = np.argsort(after)
+        result.append((size, np.take(place, after, axis).ravel(), np.take(place, before, axis).ravel()))
+    return result
+
+
+def ring(slot, axis, middle):
+    size, following, preceding = axis
+    slots = [slot]
+    forward = backward = slot
+    for _ in range((size - 1) // 2):
+        forward, backward = forward.send(following), backward.send(preceding)
+        slots += [forward, backward]
+    if size == 2:
+        slots.append(slot.send(following))
+    elif size % 2 == 0:
+        low, high = halves(forward.parts[0], middle)[0], halves(backward.parts[0], middle)[1]
+        slots.append(Slot([permute(low, following), permute(high, preceding)], moved(forward.source, following)))
+    return slots
+
+
+def slot_sources(devices):
+    result = []
+    for size, following, preceding in axes_of(devices):
+        here = np.arange(devices)
+        sources = [here]
+        forward = backward = here
+        for _ in range((size - 1) // 2):
+            forward, backward = moved(forward, following), moved(backward, preceding)
+            sources += [forward, backward]
+        if size % 2 == 0:
+            sources.append(moved(forward, following))
+        result.append(sources)
+    return result
+
+
+def gather(block, devices, middle):
+    outer, inner, core = axes_of(devices)
+    along = ring(Slot([block], np.arange(devices)), outer, middle)
+    spread = [ring(slot, inner, middle) for slot in along]
+    chip = [spread[z][y] for y in range(inner[0]) for z in range(outer[0])]
+    return chip + [slot.send(core[1]) for slot in chip]
+
+
+def give_back(pieces, devices, add):
+    outer, inner, core = slot_sources(devices)
+    pieces = pieces[None]
+    sources = [np.arange(devices)]
+    for slots in (core, inner, outer):
+        came = [pieces[:, 0]] + [permute(pieces[:, s], target) for s, target in enumerate(slots) if s]
+        if add:
+            pieces = functools.reduce(jnp.add, came)
+        else:
+            pieces = jnp.concatenate(came, 0)
+            sources = [moved(source, target) for target in slots for source in sources]
+    return pieces[0] if add else (pieces, sources)
+
+
+def norm_kernel(hidden, gain, tag, out):
+    states = hidden[...].astype(jnp.float32)
+    scale = lax.rsqrt(jnp.mean(states * states, -1, keepdims=True) + EPSILON)
+    normed = states * scale * gain[...].astype(jnp.float32)
+    steps, rows, width = normed.shape
+    rows = [normed[step, row : row + 1] for row in range(rows) for step in range(steps)]
+    out[:, :width] = jnp.concatenate(rows, 0).astype(out.dtype)
+    out[:, width:] = tag[...].astype(out.dtype)
+
+
+def norm(hidden, gain, tag):
+    steps, rows, width = hidden.shape
+    return pl.pallas_call(
+        norm_kernel,
+        out_shape=jax.ShapeDtypeStruct((steps * rows, width + TAG), jnp.bfloat16),
+        in_specs=[VMEM] * 3,
+        out_specs=VMEM,
+        compiler_params=pltpu.CompilerParams(vmem_limit_bytes=VMEM_LIMIT),
+        cost_estimate=pl.CostEstimate(flops=6 * steps * rows * width, bytes_accessed=4 * steps * rows * width, transcendentals=0),
+    )(hidden, gain.reshape(1, width), tag)
+
+
+def assemble(slots, first, width):
+    pieces = []
+    for parts in slots:
+        ref, base = parts
+        pieces.append(ref[:, pl.ds(pl.multiple_of(first - base, 128), width)].astype(jnp.float32))
+    return jnp.concatenate(pieces, 0).astype(jnp.bfloat16)
+
+
+def split_refs(shape_of_slots, refs, middle):
+    low, high, place = [], [], 0
+    for count in shape_of_slots:
+        if count == 1:
+            low.append((refs[place], 0))
+            high.append((refs[place], 0))
+        else:
+            low.append((refs[place], 0))
+            high.append((refs[place + 1], middle))
+        place += count
+    return low, high
+
+
+def stream(weights, buffers, arrived, depth):
+    def start(index, carry):
+        rows = pl.ds(pl.multiple_of(index * depth, depth), depth)
+        pltpu.make_async_copy(weights.at[rows, :], buffers.at[index], arrived.at[index]).start()
+        return carry
+
+    lax.fori_loop(0, buffers.shape[0], start, 0)
+
+
+def multiply(low, high, weights, buffers, arrived, depth, total, kept=None):
+    chunks = buffers.shape[0]
+    total[...] = jnp.zeros_like(total)
+    for which, slots in ((0, low), (1, high)):
+
+        def step(index, carry):
+            block = assemble(slots, index * depth, depth)
+            if kept is not None:
+                kept[index] = block
+            rows = pl.ds(pl.multiple_of(index * depth, depth), depth)
+            pltpu.make_async_copy(weights.at[rows, :], buffers.at[index], arrived.at[index]).wait()
+            total[...] += jnp.dot(block, buffers[index], preferred_element_type=jnp.float32)
+            return carry
+
+        lax.fori_loop(which * (chunks // 2), (which + 1) * (chunks // 2), step, 0)
+
+
+def turns(positions):
+    shape = (positions.shape[0], HD)
+    lane = lax.broadcasted_iota(jnp.int32, shape, 1)
+    pair = (lane // 2).astype(jnp.float32)
+    angles = positions * jnp.exp(pair * (-2.0 * math.log(ROPE_BASE) / HD))
+    return jnp.cos(angles), jnp.where(lane % 2 == 0, -1.0, 1.0) * jnp.sin(angles)
+
+
+def turn(values, cosine, sine):
+    lanes = values.shape[-1]
+    even = lax.broadcasted_iota(jnp.int32, values.shape, 1) % 2 == 0
+    swapped = jnp.where(even, pltpu.roll(values, lanes - 1, 1), pltpu.roll(values, 1, 1))
+    return values * cosine + swapped * sine
+
+
+def project_kernel(layout, middle, width, me, *refs):
+    count = sum(layout)
+    low, high = split_refs(layout, refs, middle)
+    weights, keyval, queries, fresh, buffers, small, kept, total, packed, arrived, came = refs[count:]
+    depth = buffers.shape[1]
+    for which in range(2):
+        pltpu.make_async_copy(keyval.at[which], small.at[which], came.at[which]).start()
+    stream(weights, buffers, arrived, depth)
+    tags = jnp.concatenate([ref[:, width - base :].astype(jnp.float32) for ref, base in high], 0)
+    cosine, sine = turns(tags[:, 0:1] * 32.0 + tags[:, 1:2])
+    multiply(low, high, weights, buffers, arrived, depth, total, kept)
+    own = kept[me[0]]
+    kv_width = keyval.shape[2]
+    for which in range(2):
+        pltpu.make_async_copy(keyval.at[which], small.at[which], came.at[which]).wait()
+        fresh[:, which * kv_width : (which + 1) * kv_width] = jnp.dot(
+            own, small[which], preferred_element_type=jnp.float32
+        )
+    heads = total.shape[1] // HD
+    for head in range(heads):
+        turned = turn(total[:, head * HD : (head + 1) * HD], cosine, sine)
+        for slot in range(packed.shape[0]):
+            for row in range(2):
+                place, at = row * 2 * heads + head * 2, slot * 4 + row * 2
+                packed[slot, place : place + 2, :] = turned[at : at + 2, :]
+    queries[...] = packed[...].astype(queries.dtype)
+
+
+def project(slots, w_query, w_keyval, me, middle):
+    devices = len(slots)
+    width, columns = w_query.shape
+    depth = w_keyval.shape[1]
+    rows = devices * slots[0].parts[0].shape[0]
+    parts = [part for slot in slots for part in slot.parts]
+    packed = (devices, rows // devices * (columns // HD), HD)
+    kv_width = w_keyval.shape[2]
+    return pl.pallas_call(
+        functools.partial(project_kernel, [len(slot.parts) for slot in slots], middle, width),
+        out_shape=[
+            jax.ShapeDtypeStruct(packed, jnp.bfloat16),
+            jax.ShapeDtypeStruct((rows, 2 * kv_width), jnp.float32),
+        ],
+        in_specs=[SMEM] + [VMEM] * len(parts) + [HBM, HBM],
+        out_specs=[VMEM, VMEM],
+        scratch_shapes=[
+            pltpu.VMEM((devices, depth, columns), w_query.dtype),
+            pltpu.VMEM((2, depth, kv_width), w_keyval.dtype),
+            pltpu.VMEM((devices, rows, depth), jnp.bfloat16),
+            pltpu.VMEM((rows, columns), jnp.float32),
+            pltpu.VMEM(packed, jnp.float32),
+            pltpu.SemaphoreType.DMA((devices,)),
+            pltpu.SemaphoreType.DMA((2,)),
+        ],
+        compiler_params=pltpu.CompilerParams(vmem_limit_bytes=VMEM_LIMIT),
+        cost_estimate=pl.CostEstimate(
+            flops=2 * rows * columns * width, bytes_accessed=2 * columns * width, transcendentals=2 * rows * HD
+        ),
+    )(me, *parts, w_query, w_keyval)
+
+
+def out_kernel(layout, middle, *refs):
+    count = sum(layout)
+    low, high = split_refs(layout, refs, middle)
+    weights, out, buffers, total, arrived = refs[count:]
+    depth = buffers.shape[1]
+    stream(weights, buffers, arrived, depth)
+    multiply(low, high, weights, buffers, arrived, depth, total)
+    own = out.shape[1]
+    for slot in range(out.shape[0]):
+        out[slot] = total[slot * own : (slot + 1) * own].astype(out.dtype)
+
+
+def project_out(slots, w_out, middle, chunks):
+    devices = len(slots)
+    width, columns = w_out.shape
+    own = slots[0].parts[0].shape[0]
+    parts = [part for slot in slots for part in slot.parts]
+    return pl.pallas_call(
+        functools.partial(out_kernel, [len(slot.parts) for slot in slots], middle),
+        out_shape=jax.ShapeDtypeStruct((devices, own, columns), jnp.bfloat16),
+        in_specs=[VMEM] * len(parts) + [HBM],
+        out_specs=VMEM,
+        scratch_shapes=[
+            pltpu.VMEM((chunks, width // chunks, columns), w_out.dtype),
+            pltpu.VMEM((devices * own, columns), jnp.float32),
+            pltpu.SemaphoreType.DMA((chunks,)),
+        ],
+        compiler_params=pltpu.CompilerParams(vmem_limit_bytes=VMEM_LIMIT),
+        cost_estimate=pl.CostEstimate(
+            flops=2 * devices * own * columns * width, bytes_accessed=2 * columns * width, transcendentals=0
+        ),
+    )(*parts, w_out)
+
+
+def attend_kernel(
+    devices, kv_heads, length, lengths, sources, pieces, fresh, cache, out, keys, values, queries, mixed, arrived
+):
+    padded = keys.shape[1]
+    width = kv_heads * HD
+    tile = pieces.shape[1] // 2
+    per_head = devices // kv_heads * tile
+    scale = 1.0 / math.sqrt(HD)
+    copies = []
+    for row in range(2):
+        for which, target in enumerate((keys, values)):
+            copies.append(
+                pltpu.make_async_copy(cache.at[which, row], target.at[row, pl.ds(0, length), :], arrived.at[2 * row + which])
+            )
+            copies[-1].start()
+    for slot in range(devices):
+        queries[sources[slot]] = pieces[slot].astype(jnp.float32)
+    line = lax.broadcasted_iota(jnp.int32, (8, 1), 0)
+    first = jnp.where(line < 2, lengths[0], lengths[1])
+    cosine, sine = turns((first + line % 2).astype(jnp.float32))
+    total = fresh[...]
+    total = jnp.concatenate([total, total], 0)
+    new_values = total[:, width:]
+    new_keys = jnp.concatenate([turn(total[:, head * HD : (head + 1) * HD], cosine, sine) for head in range(kv_heads)], 1)
+    place = lax.broadcasted_iota(jnp.int32, (padded - length, width), 0)
+    for row in range(2):
+        for new, target in ((new_keys, keys), (new_values, values)):
+            spread = jnp.where(place == 0, new[2 * row : 2 * row + 1, :], 0.0)
+            spread = jnp.where(place == 1, new[2 * row + 1 : 2 * row + 2, :], spread)
+            target[row, length:, :] = spread.astype(target.dtype)
+    every = queries[...]
+    column = lax.broadcasted_iota(jnp.int32, (kv_heads * per_head, padded), 1)
+    step = lax.broadcasted_iota(jnp.int32, (kv_heads * per_head, padded), 0) % 2
+    for row in range(2):
+        mine = every[:, row * tile : row * tile + tile, :].reshape(kv_heads * per_head, HD)
+        spread = jnp.concatenate([mine] * kv_heads, 1)
+        own_row = lax.broadcasted_iota(jnp.int32, spread.shape, 0) // per_head
+        own_lane = lax.broadcasted_iota(jnp.int32, spread.shape, 1) // HD
+        spread = jnp.where(own_row == own_lane, spread, 0.0).astype(jnp.bfloat16)
+        copies[2 * row].wait()
+        scores = lax.dot_general(spread, keys[row], (((1,), (1,)), ((), ())), preferred_element_type=jnp.float32) * scale
+        valid = (column < lengths[row]) | ((column >= length) & (column <= length + step))
+        scores = jnp.where(valid, scores, -jnp.inf)
+        peak = jnp.max(scores, 1, keepdims=True)
+        weight = jnp.exp(scores - peak)
+        denominator = jnp.sum(weight, 1, keepdims=True)
+        copies[2 * row + 1].wait()
+        result = jnp.dot(weight.astype(jnp.bfloat16), values[row], preferred_element_type=jnp.float32)
+        for head in range(kv_heads):
+            rows = slice(head * per_head, (head + 1) * per_head)
+            part = result[rows, head * HD : (head + 1) * HD] / denominator[rows]
+            for query in range(per_head // 2):
+                lanes = slice((head * per_head // 2 + query) * HD, (head * per_head // 2 + query + 1) * HD)
+                for at in range(2):
+                    mixed[at * 2 + row : at * 2 + row + 1, lanes] = part[2 * query + at : 2 * query + at + 1]
+    out[...] = mixed[...].astype(out.dtype)
+
+
+def attend(pieces, fresh, cache, lengths, sources):
+    devices = pieces.shape[0]
+    length, width = cache.shape[2], cache.shape[3]
+    padded = length + HD
+    rows, heads = fresh.shape[0], devices * pieces.shape[1] // fresh.shape[0]
+    return pl.pallas_call(
+        functools.partial(attend_kernel, devices, width // HD, length),
+        out_shape=jax.ShapeDtypeStruct((rows, heads * HD), jnp.bfloat16),
+        in_specs=[SMEM, SMEM, VMEM, VMEM, HBM],
+        out_specs=VMEM,
+        scratch_shapes=[
+            pltpu.VMEM((2, padded, width), cache.dtype),
+            pltpu.VMEM((2, padded, width), cache.dtype),
+            pltpu.VMEM(pieces.shape, jnp.float32),
+            pltpu.VMEM((rows, heads * HD), jnp.float32),
+            pltpu.SemaphoreType.DMA((4,)),
+        ],
+        compiler_params=pltpu.CompilerParams(vmem_limit_bytes=VMEM_LIMIT),
+        cost_estimate=pl.CostEstimate(
+            flops=8 * 128 * padded * width, bytes_accessed=8 * length * width, transcendentals=256 * padded
+        ),
+    )(lengths, sources, pieces, fresh, cache)
+
+
+def finish_kernel(sources, pieces, out):
+    columns = pieces.shape[2]
+    steps, rows = out.shape[:2]
+    for slot in range(pieces.shape[0]):
+        lanes = pl.ds(pl.multiple_of(sources[slot] * columns, columns), columns)
+        piece = pieces[slot].astype(jnp.float32)
+        for step in range(steps):
+            out[step, :, lanes] = piece[step * rows : (step + 1) * rows].astype(out.dtype)
+
+
+def finish(pieces, sources, steps):
+    devices, own, columns = pieces.shape
+    return pl.pallas_call(
+        finish_kernel,
+        out_shape=jax.ShapeDtypeStruct((steps, own // steps, devices * columns), jnp.bfloat16),
+        in_specs=[SMEM, VMEM],
+        out_specs=VMEM,
+        compiler_params=pltpu.CompilerParams(vmem_limit_bytes=VMEM_LIMIT),
+    )(sources, pieces)
+
+
+def body(hidden, norm_gain, w_query, w_keyval, w_out, kv_cache, lengths):
+    steps, rows, width = hidden.shape
+    devices = lax.axis_size("gx")
+    me = lax.axis_index("gx")
+    outer, inner, core = axes_of(devices)
+    grid = (core[0], inner[0], outer[0])
+
+    positions = (lengths[:, None] + jnp.arange(steps, dtype=jnp.int32)[None, :]).reshape(rows * steps, 1)
+    lane = jnp.arange(TAG)[None, :]
+    tag = jnp.where(lane == 0, positions // 32, jnp.where(lane == 1, positions % 32, 0)).astype(jnp.float32)
+
+    slots = gather(norm(hidden, norm_gain, tag), devices, width // 2)
+    queries, fresh = project(slots, w_query, w_keyval, me.reshape(1), width // 2)
+    queries, order = give_back(queries.reshape(*grid, *queries.shape[1:]), devices, False)
+    fresh = give_back(fresh.reshape(*grid, rows * steps, fresh.shape[1]), devices, True)
+    sources = lax.dynamic_index_in_dim(jnp.asarray(np.stack(order, 1).astype(np.int32)), me, 0, keepdims=False)
+
+    mixed = attend(queries, fresh, kv_cache, lengths, sources)
+    slots = gather(mixed, devices, mixed.shape[1] // 2)
+    columns = project_out(slots, w_out, mixed.shape[1] // 2, devices // 2)
+    columns, _ = give_back(columns.reshape(*grid, *columns.shape[1:]), devices, False)
+    return finish(columns, sources, steps)
 
 
 def rotate(values, positions):
@@ -32,7 +441,7 @@
     return turned.reshape(row_total, head_count, head_width)
 
 
-def attend(queries, cache_keys, cache_values, lengths, fresh_keys, fresh_values):
+def attend_split_heads(queries, cache_keys, cache_values, lengths, fresh_keys, fresh_values):
     score_scale = 1.0 / math.sqrt(HD)
     fresh_scores = (
         jnp.einsum("rkgd,rskd->rkgs", queries, fresh_keys, preferred_element_type=jnp.float32)
@@ -63,7 +472,7 @@
     return (mixed / denominator[..., None]).astype(jnp.bfloat16)
 
 
-def body(hidden, norm_gain, w_query, w_keyval, w_out, kv_cache, lengths):
+def body_split_heads(hidden, norm_gain, w_query, w_keyval, w_out, kv_cache, lengths):
     step_count, rows_dev, model_width = hidden.shape
     devices = lax.axis_size("gx")
     device_index = lax.axis_index("gx")
@@ -108,7 +517,7 @@
         queries, key_new, value_new = (prepare_queries, key_new, value_new)
         new_keys.append(key_new)
         new_values.append(value_new)
-        mixed = attend(
+        mixed = attend_split_heads(
             queries,
             cache_keys,
             cache_values,
@@ -126,6 +535,12 @@
 
 
 def solution(mesh):
+    devices = mesh.shape["gx"]
+
+    def run(*arrays):
+        whole_heads = arrays[2].shape[1] % HD == 0 and devices % 2 == 0
+        return (body if whole_heads else body_split_heads)(*arrays)
+
     in_specs = (
         P(None, ("group", "gx"), None),
         P(),
@@ -136,4 +551,4 @@
         P(("group", "gx")),
     )
     out_specs = P(None, ("group", "gx"), None)
-    return jax.shard_map(body, mesh=mesh, in_specs=in_specs, out_specs=out_specs, check_vma=False)
+    return jax.shard_map(run, mesh=mesh, in_specs=in_specs, out_specs=out_specs, check_vma=False)

time: 315 us -> 104 us (0.33)
  waiting for transfers between devices: 93.2 us -> 30 us
  local copies, waits for them, and re-layouts: 67.3 us -> 6.48 us
  blocking collectives: 55.2 us -> 0 us
  matrix products: 46 us -> 0 us
  starting transfers between devices: 10.8 us -> 46.9 us
  other arithmetic: 26.8 us -> 1.26 us
  Pallas kernels: 0 us -> 18.9 us
  between operations: 14.1 us -> 0.23 us
    all_gather x2 -> x0, waiting for transfers between devices: 59.8 us -> none  [body(): shard_piece = lax.all_gather(normed[step_index], 'gx', axis=0, tiled=True)]
    ppermute x0 -> x53, starting transfers between devices: none -> 46.9 us  [permute(): lax.ppermute(block, 'gx', [(int(i), int(t)) for i, t in enumerate(target)])]
    dot_general x13 -> x0, matrix products: 46 us -> none  [the longest x2 19 us: body(): queries = jnp.dot(shard_piece, w_query, preferred_element_type=jnp.float32)]
    all_gather x2 -> x0, blocking collectives: 45.8 us -> none  [body(): lax.all_gather(mixed.reshape(rows_dev, heads_width), 'gx', axis=0, tiled=...]
    unnamed x4 -> x0, waiting for transfers between devices: 33.3 us -> none
    mul x16 -> x0, local copies, waits for them, and re-layouts: 32.5 us -> none  [the longest x4 8.16 us: rotate(): second_half * sine_part]
    ppermute x0 -> x53, waiting for transfers between devices: none -> 30 us  [permute(): lax.ppermute(block, 'gx', [(int(i), int(t)) for i, t in enumerate(target)])]
    mul x2 -> x0, other arithmetic: 22 us -> none  [rotate(): second_half * sine_part]
  transfers between devices with their start and end apart: 6 -> 53, of which waited for: 3 -> 21; matrix products, arithmetic and copies ran while one was open for 34% -> 1% of each run, Pallas kernels for 0% -> 0%
where the time goes in v1:
time: 104 us
  starting transfers between devices  46.9 us (45%)
  waiting for transfers between devices  30 us (29%)
  Pallas kernels  18.9 us (18%)
  local copies, waits for them, and re-layouts  6.48 us (6%)
  other arithmetic  1.26 us (1%)
    ppermute x53, starting transfers between devices, permute(): lax.ppermute(block, 'gx', [(int(i), int(t)) for i, t in enumerate(target)])  46.9 us
    ppermute x53, waiting for transfers between devices, permute(): lax.ppermute(block, 'gx', [(int(i), int(t)) for i, t in enumerate(target)])  30 us
    pallas_call x1, Pallas kernels, project(): pl.pallas_call(functools.partial(project_kernel, [len(slot.parts) for slo...  7.49 us
    pallas_call x1, Pallas kernels, project_out(): pl.pallas_call(functools.partial(out_kernel, [len(slot.parts) for slot in...  6.44 us
    unnamed x8, local copies, waits for them, and re-layouts  4.68 us
    pallas_call x1, Pallas kernels, attend(): pl.pallas_call(functools.partial(attend_kernel, devices, width // HD, len...  3.21 us
  transfers between devices with their start and end apart: 53, of which 21 were waited for; matrix products, arithmetic and copies ran while one was open for 1% of the time, Pallas kernels for 0%

profile of v1, /device:TPU:0, one launch (start us, length us, event | category | flops | bytes accessed | tf_op | source)
XLA Modules:
  0.0 103.8 jit_solution(10693935076044100119)
XLA Ops:
  3.2 4.1 %collective-permute-start = (bf16[4,16512]{1,0:T(4,128)(2,1)S(1)}, bf16[4,16512]{1,0:T(4,128)(2,1)S(1)}, u32[]{:S(2)}, u32[]{:S(2)}) collective-permute-start(bf16[4,16512]{1,0:T(4,128)(2,1)S(1)} %shard_map.82.refs_0_), channel_id=1, source_target_pairs={{0,8},{1,9},{2,10},{3,11},{4,0},{5,1},{6,2},{7,3},{8,12},{9,13},{1... | collective-permute-start | bytes 396296 | tf_op jit(solution)/shard_map/ppermute | solution.py:23
  8.8 2.4 %collective-permute-done.refs_1_ = bf16[4,16512]{1,0:T(4,128)(2,1)S(1)} collective-permute-done((bf16[4,16512]{1,0:T(4,128)(2,1)S(1)}, bf16[4,16512]{1,0:T(4,128)(2,1)S(1)}, u32[]{:S(2)}, u32[]{:S(2)}) %collective-permute-start) | collective-permute-done | bytes 132128 | tf_op jit(solution)/shard_map/ppermute | solution.py:23
  11.2 3.4 %collective-permute-start.2 = (bf16[4,8192]{1,0:T(4,128)(2,1)S(1)}, bf16[4,8192]{1,0:T(4,128)(2,1)S(1)}, u32[]{:S(2)}, u32[]{:S(2)}) collective-permute-start(bf16[4,8192]{1,0:T(4,128)(2,1)S(1)} %slice.112), channel_id=1, source_target_pairs={{0,8},{1,9},{2,10},{3,11},{4,0},{5,1},{6,2},{7,3},{8,12},{9,13},{1... | collective-permute-start | bytes 196616 | tf_op jit(solution)/shard_map/ppermute | solution.py:23
  20.2 2.5 %collective-permute-done.7.refs_8_ = bf16[4,8192]{1,0:T(4,128)(2,1)S(1)} collective-permute-done((bf16[4,8192]{1,0:T(4,128)(2,1)S(1)}, bf16[4,8192]{1,0:T(4,128)(2,1)S(1)}, u32[]{:S(2)}, u32[]{:S(2)}) %collective-permute-start.7) | collective-permute-done | bytes 65568 | tf_op jit(solution)/shard_map/ppermute | solution.py:23
  25.3 2.2 %collective-permute-done.8.refs_9_ = bf16[4,8320]{1,0:T(4,128)(2,1)S(1)} collective-permute-done((bf16[4,8320]{1,0:T(4,128)(2,1)S(1)}, bf16[4,8320]{1,0:T(4,128)(2,1)S(1)}, u32[]{:S(2)}, u32[]{:S(2)}) %collective-permute-start.8) | collective-permute-done | bytes 66592 | tf_op jit(solution)/shard_map/ppermute | solution.py:23
  28.9 1.6 %copy-done.1 = bf16[2,1024,512]{2,1,0:T(8,128)(2,1)S(1)} copy-done((bf16[2,1024,512]{2,1,0:T(8,128)(2,1)S(1)}, bf16[2,1024,512]{2,1,0:T(8,128)(2,1)}, u32[]{:S(2)}) %copy-start.1) | copy-done | bytes 2097176
  30.5 7.5 %shard_map.83 = (bf16[16,16,128]{2,1,0:T(8,128)(2,1)S(1)}, f32[64,1024]{1,0:T(8,128)S(1)}) custom-call(s32[1]{0:T(128)} %bitcast.1.me, bf16[4,16512]{1,0:T(4,128)(2,1)S(1)} %shard_map.82.refs_0_, bf16[4,16512]{1,0:T(4,128)(2,1)S(1)} %collective-permute-done.refs_1_, bf16[4,16512]{1,0:T(4,128)(2,1)S(1)} %collective-permute-done.1.refs_2_, ...), custom_call_target="tpu_custom_call" | custom-call | flops 1073741824 | bytes 16777216 | tf_op jit(solution)/shard_map/pallas_call | solution.py:239
  39.7 1.6 %collective-permute-start.20 = (bf16[2,4,16,128]{3,2,0,1:T(8,128)(2,1)S(1)}, bf16[2,4,16,128]{3,2,0,1:T(8,128)(2,1)S(1)}, u32[]{:S(2)}, u32[]{:S(2)}) collective-permute-start(bf16[2,4,16,128]{3,2,0,1:T(8,128)(2,1)S(1)} %get-tuple-element.25), channel_id=1, source_target_pairs={{0,2},{1,3},{2,0},{3,1},{4,6},{5,7},{6,4},{7,5},{8,10},{9,11},{10,... | collective-permute-start | bytes 98312 | tf_op jit(solution)/shard_map/ppermute | solution.py:23
  41.9 1.8 %collective-permute-done.20 = bf16[2,4,16,128]{3,2,0,1:T(8,128)(2,1)S(1)} collective-permute-done((bf16[2,4,16,128]{3,2,0,1:T(8,128)(2,1)S(1)}, bf16[2,4,16,128]{3,2,0,1:T(8,128)(2,1)S(1)}, u32[]{:S(2)}, u32[]{:S(2)}) %collective-permute-start.20) | collective-permute-done | bytes 32800 | tf_op jit(solution)/shard_map/ppermute | solution.py:23
  43.7 3.3 %collective-permute-start.21 = (bf16[4,16,128]{2,1,0:T(8,128)(2,1)S(1)}, bf16[4,16,128]{2,1,0:T(8,128)(2,1)S(1)}, u32[]{:S(2)}, u32[]{:S(2)}) collective-permute-start(bf16[4,16,128]{2,1,0:T(8,128)(2,1)S(1)} %get-tuple-element.21), channel_id=1, source_target_pairs={{0,4},{1,5},{2,6},{3,7},{4,12},{5,13},{6,14},{7,15},{8,0},{9,1},{1... | collective-permute-start | bytes 49160 | tf_op jit(solution)/shard_map/ppermute | solution.py:23
  47.0 2.4 %collective-permute-start.23 = (bf16[4,16,128]{2,1,0:T(8,128)(2,1)S(1)}, bf16[4,16,128]{2,1,0:T(8,128)(2,1)S(1)}, u32[]{:S(2)}, u32[]{:S(2)}) collective-permute-start(bf16[4,16,128]{2,1,0:T(8,128)(2,1)S(1)} %get-tuple-element.22), channel_id=1, source_target_pairs={{0,12},{1,13},{2,14},{3,15},{4,8},{5,9},{6,10},{7,11},{8,4},{9,5},... | collective-permute-start | bytes 49160 | tf_op jit(solution)/shard_map/ppermute | solution.py:23
  49.5 2.9 %collective-permute-start.27 = (f32[1,4,1024]{2,1,0:T(4,128)S(1)}, f32[1,4,1024]{2,1,0:T(4,128)S(1)}, u32[]{:S(2)}, u32[]{:S(2)}) collective-permute-start(f32[1,4,1024]{2,1,0:T(4,128)S(1)} %get-tuple-element.19), channel_id=1, source_target_pairs={{0,8},{1,9},{2,10},{3,11},{4,0},{5,1},{6,2},{7,3},{8,12},{9,13},{1... | collective-permute-start | bytes 49160 | tf_op jit(solution)/shard_map/ppermute | solution.py:23
  54.2 3.8 %collective-permute-done.28 = f32[1,4,1024]{2,1,0:T(4,128)S(1)} collective-permute-done((f32[1,4,1024]{2,1,0:T(4,128)S(1)}, f32[1,4,1024]{2,1,0:T(4,128)S(1)}, u32[]{:S(2)}, u32[]{:S(2)}) %collective-permute-start.28) | collective-permute-done | bytes 16416 | tf_op jit(solution)/shard_map/ppermute | solution.py:23
  58.0 2.2 %copy-done = bf16[2,2,1024,512]{3,2,1,0:T(8,128)(2,1)S(1)} copy-done((bf16[2,2,1024,512]{3,2,1,0:T(8,128)(2,1)S(1)}, bf16[2,2,1024,512]{3,2,1,0:T(8,128)(2,1)}, u32[]{:S(2)}) %copy-start) | copy-done | bytes 4194328
  60.2 3.2 %shard_map.84.refs_0_ = bf16[4,8192]{1,0:T(4,128)(2,1)S(1)} custom-call(s32[2]{0:T(128)S(1)} %copy-done.3, s32[16]{0:T(128)S(1)} %dynamic-slice_bitcast_fusion.sources, bf16[16,16,128]{2,1,0:T(8,128)(2,1)S(1)} %pad_maximum_fusion.2.pieces, f32[4,1024]{1,0:T(4,128)S(1)} %fusion.24.fresh, bf16[2,2,1024,512]{3,2,1,0:T(8,128)(2,1)S(1)} %copy-done), custom_call_target="tpu_custom_call" | custom-call | flops 603979776 | bytes 4194304 | tf_op jit(solution)/shard_map/pallas_call | solution.py:360
  63.5 2.0 %collective-permute-start.30 = (bf16[4,8192]{1,0:T(4,128)(2,1)S(1)}, bf16[4,8192]{1,0:T(4,128)(2,1)S(1)}, u32[]{:S(2)}, u32[]{:S(2)}) collective-permute-start(bf16[4,8192]{1,0:T(4,128)(2,1)S(1)} %shard_map.84.refs_0_), channel_id=1, source_target_pairs={{0,4},{1,5},{2,6},{3,7},{4,12},{5,13},{6,14},{7,15},{8,0},{9,1},{1... | collective-permute-start | bytes 196616 | tf_op jit(solution)/shard_map/ppermute | solution.py:23
  65.5 1.8 %collective-permute-start.33 = (bf16[4,8192]{1,0:T(4,128)(2,1)S(1)}, bf16[4,8192]{1,0:T(4,128)(2,1)S(1)}, u32[]{:S(2)}, u32[]{:S(2)}) collective-permute-start(bf16[4,8192]{1,0:T(4,128)(2,1)S(1)} %shard_map.84.refs_0_), channel_id=1, source_target_pairs={{0,2},{1,3},{2,0},{3,1},{4,6},{5,7},{6,4},{7,5},{8,10},{9,11},{10,... | collective-permute-start | bytes 196616 | tf_op jit(solution)/shard_map/ppermute | solution.py:23
  69.9 1.8 %collective-permute-start.34 = (bf16[4,8192]{1,0:T(4,128)(2,1)S(1)}, bf16[4,8192]{1,0:T(4,128)(2,1)S(1)}, u32[]{:S(2)}, u32[]{:S(2)}) collective-permute-start(bf16[4,8192]{1,0:T(4,128)(2,1)S(1)} %collective-permute-done.29.refs_1_), channel_id=1, source_target_pairs={{0,2},{1,3},{2,0},{3,1},{4,6},{5,7},{6,4},{7,5},{8,10},{9,11},{10,... | collective-permute-start | bytes 196616 | tf_op jit(solution)/shard_map/ppermute | solution.py:23
  74.2 1.8 %collective-permute-start.36 = (bf16[4,4096]{1,0:T(4,128)(2,1)S(1)}, bf16[4,4096]{1,0:T(4,128)(2,1)S(1)}, u32[]{:S(2)}, u32[]{:S(2)}) collective-permute-start(bf16[4,4096]{1,0:T(4,128)(2,1)S(1)} %collective-permute-done.31.refs_3_), channel_id=1, source_target_pairs={{0,2},{1,3},{2,0},{3,1},{4,6},{5,7},{6,4},{7,5},{8,10},{9,11},{10,... | collective-permute-start | bytes 98312 | tf_op jit(solution)/shard_map/ppermute | solution.py:23
  78.1 1.8 %collective-permute-done.37.refs_9_ = bf16[4,4096]{1,0:T(4,128)(2,1)S(1)} collective-permute-done((bf16[4,4096]{1,0:T(4,128)(2,1)S(1)}, bf16[4,4096]{1,0:T(4,128)(2,1)S(1)}, u32[]{:S(2)}, u32[]{:S(2)}) %collective-permute-start.37) | collective-permute-done | bytes 32800 | tf_op jit(solution)/shard_map/ppermute | solution.py:23
  81.3 6.4 %shard_map.85 = bf16[16,4,1024]{2,1,0:T(4,128)(2,1)S(1)} custom-call(bf16[4,8192]{1,0:T(4,128)(2,1)S(1)} %shard_map.84.refs_0_, bf16[4,8192]{1,0:T(4,128)(2,1)S(1)} %collective-permute-done.29.refs_1_, bf16[4,8192]{1,0:T(4,128)(2,1)S(1)} %collective-permute-done.30.refs_2_, bf16[4,4096]{1,0:T(4,128)(2,1)S(1)} %collective-permute-done.31.refs_3_, ...), custom_call_target="tpu_custom_call" | custom-call | flops 1073741824 | bytes 16777216 | tf_op jit(solution)/shard_map/pallas_call | solution.py:280
  90.0 3.7 %collective-permute-done.49 = bf16[2,4,4,1024]{3,2,0,1:T(4,128)(2,1)S(1)} collective-permute-done((bf16[2,4,4,1024]{3,2,0,1:T(4,128)(2,1)S(1)}, bf16[2,4,4,1024]{3,2,0,1:T(4,128)(2,1)S(1)}, u32[]{:S(2)}, u32[]{:S(2)}) %collective-permute-start.49) | collective-permute-done | bytes 65568 | tf_op jit(solution)/shard_map/ppermute | solution.py:23
  94.7 2.0 %collective-permute-start.51 = (bf16[4,4,1024]{2,1,0:T(4,128)(2,1)S(1)}, bf16[4,4,1024]{2,1,0:T(4,128)(2,1)S(1)}, u32[]{:S(2)}, u32[]{:S(2)}) collective-permute-start(bf16[4,4,1024]{2,1,0:T(4,128)(2,1)S(1)} %get-tuple-element.12), channel_id=1, source_target_pairs={{0,8},{1,9},{2,10},{3,11},{4,0},{5,1},{6,2},{7,3},{8,12},{9,13},{1... | collective-permute-start | bytes 98312 | tf_op jit(solution)/shard_map/ppermute | solution.py:23
  99.0 3.4 %collective-permute-done.52 = bf16[4,4,1024]{2,1,0:T(4,128)(2,1)S(1)} collective-permute-done((bf16[4,4,1024]{2,1,0:T(4,128)(2,1)S(1)}, bf16[4,4,1024]{2,1,0:T(4,128)(2,1)S(1)}, u32[]{:S(2)}, u32[]{:S(2)}) %collective-permute-start.52) | collective-permute-done | bytes 32800 | tf_op jit(solution)/shard_map/ppermute | solution.py:23
  (121 shorter events, 34.1 us)
Async XLA Ops:
  3.2 8.0 %collective-permute-start = (bf16[4,16512]{1,0:T(4,128)(2,1)S(1)}, bf16[4,16512]{1,0:T(4,128)(2,1)S(1)}, u32[]{:S(2)}, u32[]{:S(2)}) collective-permute-start(bf16[4,16512]{1,0:T(4,128)(2,1)S(1)} %shard_map.82.refs_0_), channel_id=1, source_target_pairs={{0,8},{1,9},{2,10},{3,11},{4,0},{5,1},{6,2},{7,3},{8,12},{9,13},{1... | collective-permute-start | bytes 396296 | tf_op jit(solution)/shard_map/ppermute | solution.py:23
  7.2 7.7 %collective-permute-start.1 = (bf16[4,16512]{1,0:T(4,128)(2,1)S(1)}, bf16[4,16512]{1,0:T(4,128)(2,1)S(1)}, u32[]{:S(2)}, u32[]{:S(2)}) collective-permute-start(bf16[4,16512]{1,0:T(4,128)(2,1)S(1)} %shard_map.82.refs_0_), channel_id=1, source_target_pairs={{0,4},{1,5},{2,6},{3,7},{4,12},{5,13},{6,14},{7,15},{8,0},{9,1},{1... | collective-permute-start | bytes 396296 | tf_op jit(solution)/shard_map/ppermute | solution.py:23
  7.3 10.8 %collective-permute-start.4 = (bf16[4,16512]{1,0:T(4,128)(2,1)S(1)}, bf16[4,16512]{1,0:T(4,128)(2,1)S(1)}, u32[]{:S(2)}, u32[]{:S(2)}) collective-permute-start(bf16[4,16512]{1,0:T(4,128)(2,1)S(1)} %shard_map.82.refs_0_), channel_id=1, source_target_pairs={{0,2},{1,3},{2,0},{3,1},{4,6},{5,7},{6,4},{7,5},{8,10},{9,11},{10,... | collective-permute-start | bytes 396296 | tf_op jit(solution)/shard_map/ppermute | solution.py:23
  8.8 10.4 %collective-permute-start.9 = (bf16[4,16512]{1,0:T(4,128)(2,1)S(1)}, bf16[4,16512]{1,0:T(4,128)(2,1)S(1)}, u32[]{:S(2)}, u32[]{:S(2)}) collective-permute-start(bf16[4,16512]{1,0:T(4,128)(2,1)S(1)} %shard_map.82.refs_0_), channel_id=1, source_target_pairs={{0,1},{1,0},{2,3},{3,2},{4,5},{5,4},{6,7},{7,6},{8,9},{9,8},{10,11... | collective-permute-start | bytes 396296 | tf_op jit(solution)/shard_map/ppermute | solution.py:23
  11.2 6.0 %collective-permute-start.2 = (bf16[4,8192]{1,0:T(4,128)(2,1)S(1)}, bf16[4,8192]{1,0:T(4,128)(2,1)S(1)}, u32[]{:S(2)}, u32[]{:S(2)}) collective-permute-start(bf16[4,8192]{1,0:T(4,128)(2,1)S(1)} %slice.112), channel_id=1, source_target_pairs={{0,8},{1,9},{2,10},{3,11},{4,0},{5,1},{6,2},{7,3},{8,12},{9,13},{1... | collective-permute-start | bytes 196616 | tf_op jit(solution)/shard_map/ppermute | solution.py:23
  15.0 5.2 %collective-permute-start.3 = (bf16[4,8320]{1,0:T(4,128)(2,1)S(1)}, bf16[4,8320]{1,0:T(4,128)(2,1)S(1)}, u32[]{:S(2)}, u32[]{:S(2)}) collective-permute-start(bf16[4,8320]{1,0:T(4,128)(2,1)S(1)} %slice.113), channel_id=1, source_target_pairs={{0,4},{1,5},{2,6},{3,7},{4,12},{5,13},{6,14},{7,15},{8,0},{9,1},{1... | collective-permute-start | bytes 199688 | tf_op jit(solution)/shard_map/ppermute | solution.py:23
  15.6 7.5 %collective-permute-start.5 = (bf16[4,16512]{1,0:T(4,128)(2,1)S(1)}, bf16[4,16512]{1,0:T(4,128)(2,1)S(1)}, u32[]{:S(2)}, u32[]{:S(2)}) collective-permute-start(bf16[4,16512]{1,0:T(4,128)(2,1)S(1)} %collective-permute-done.refs_1_), channel_id=1, source_target_pairs={{0,2},{1,3},{2,0},{3,1},{4,6},{5,7},{6,4},{7,5},{8,10},{9,11},{10,... | collective-permute-start | bytes 396296 | tf_op jit(solution)/shard_map/ppermute | solution.py:23
  17.2 5.5 %collective-permute-start.7 = (bf16[4,8192]{1,0:T(4,128)(2,1)S(1)}, bf16[4,8192]{1,0:T(4,128)(2,1)S(1)}, u32[]{:S(2)}, u32[]{:S(2)}) collective-permute-start(bf16[4,8192]{1,0:T(4,128)(2,1)S(1)} %collective-permute-done.2.refs_3_), channel_id=1, source_target_pairs={{0,2},{1,3},{2,0},{3,1},{4,6},{5,7},{6,4},{7,5},{8,10},{9,11},{10,... | collective-permute-start | bytes 196616 | tf_op jit(solution)/shard_map/ppermute | solution.py:23
  18.1 6.6 %collective-permute-start.6 = (bf16[4,16512]{1,0:T(4,128)(2,1)S(1)}, bf16[4,16512]{1,0:T(4,128)(2,1)S(1)}, u32[]{:S(2)}, u32[]{:S(2)}) collective-permute-start(bf16[4,16512]{1,0:T(4,128)(2,1)S(1)} %collective-permute-done.1.refs_2_), channel_id=1, source_target_pairs={{0,2},{1,3},{2,0},{3,1},{4,6},{5,7},{6,4},{7,5},{8,10},{9,11},{10,... | collective-permute-start | bytes 396296 | tf_op jit(solution)/shard_map/ppermute | solution.py:23
  19.2 5.5 %collective-permute-start.10 = (bf16[4,16512]{1,0:T(4,128)(2,1)S(1)}, bf16[4,16512]{1,0:T(4,128)(2,1)S(1)}, u32[]{:S(2)}, u32[]{:S(2)}) collective-permute-start(bf16[4,16512]{1,0:T(4,128)(2,1)S(1)} %collective-permute-done.refs_1_), channel_id=1, source_target_pairs={{0,1},{1,0},{2,3},{3,2},{4,5},{5,4},{6,7},{7,6},{8,9},{9,8},{10,11... | collective-permute-start | bytes 396296 | tf_op jit(solution)/shard_map/ppermute | solution.py:23
  22.7 4.8 %collective-permute-start.14 = (bf16[4,16512]{1,0:T(4,128)(2,1)S(1)}, bf16[4,16512]{1,0:T(4,128)(2,1)S(1)}, u32[]{:S(2)}, u32[]{:S(2)}) collective-permute-start(bf16[4,16512]{1,0:T(4,128)(2,1)S(1)} %collective-permute-done.4.refs_5_), channel_id=1, source_target_pairs={{0,1},{1,0},{2,3},{3,2},{4,5},{5,4},{6,7},{7,6},{8,9},{9,8},{10,11... | collective-permute-start | bytes 396296 | tf_op jit(solution)/shard_map/ppermute | solution.py:23
  41.4 8.1 %collective-permute-start.25 = (f32[1,4,4,1024]{3,2,1,0:T(4,128)S(1)}, f32[1,4,4,1024]{3,2,1,0:T(4,128)S(1)}, u32[]{:S(2)}, u32[]{:S(2)}) collective-permute-start(f32[1,4,4,1024]{3,2,1,0:T(4,128)S(1)} %slice_bitcast_fusion.4), channel_id=1, source_target_pairs={{0,2},{1,3},{2,0},{3,1},{4,6},{5,7},{6,4},{7,5},{8,10},{9,11},{10,... | collective-permute-start | bytes 196616 | tf_op jit(solution)/shard_map/ppermute | solution.py:23
  43.7 8.7 %collective-permute-start.21 = (bf16[4,16,128]{2,1,0:T(8,128)(2,1)S(1)}, bf16[4,16,128]{2,1,0:T(8,128)(2,1)S(1)}, u32[]{:S(2)}, u32[]{:S(2)}) collective-permute-start(bf16[4,16,128]{2,1,0:T(8,128)(2,1)S(1)} %get-tuple-element.21), channel_id=1, source_target_pairs={{0,4},{1,5},{2,6},{3,7},{4,12},{5,13},{6,14},{7,15},{8,0},{9,1},{1... | collective-permute-start | bytes 49160 | tf_op jit(solution)/shard_map/ppermute | solution.py:23
  47.0 6.9 %collective-permute-start.22 = (bf16[4,16,128]{2,1,0:T(8,128)(2,1)S(1)}, bf16[4,16,128]{2,1,0:T(8,128)(2,1)S(1)}, u32[]{:S(2)}, u32[]{:S(2)}) collective-permute-start(bf16[4,16,128]{2,1,0:T(8,128)(2,1)S(1)} %get-tuple-element.23), channel_id=1, source_target_pairs={{0,8},{1,9},{2,10},{3,11},{4,0},{5,1},{6,2},{7,3},{8,12},{9,13},{1... | collective-permute-start | bytes 49160 | tf_op jit(solution)/shard_map/ppermute | solution.py:23
  47.0 6.9 %collective-permute-start.23 = (bf16[4,16,128]{2,1,0:T(8,128)(2,1)S(1)}, bf16[4,16,128]{2,1,0:T(8,128)(2,1)S(1)}, u32[]{:S(2)}, u32[]{:S(2)}) collective-permute-start(bf16[4,16,128]{2,1,0:T(8,128)(2,1)S(1)} %get-tuple-element.22), channel_id=1, source_target_pairs={{0,12},{1,13},{2,14},{3,15},{4,8},{5,9},{6,10},{7,11},{8,4},{9,5},... | collective-permute-start | bytes 49160 | tf_op jit(solution)/shard_map/ppermute | solution.py:23
  49.5 4.7 %collective-permute-start.26 = (f32[1,4,1024]{2,1,0:T(4,128)S(1)}, f32[1,4,1024]{2,1,0:T(4,128)S(1)}, u32[]{:S(2)}, u32[]{:S(2)}) collective-permute-start(f32[1,4,1024]{2,1,0:T(4,128)S(1)} %get-tuple-element.17), channel_id=1, source_target_pairs={{0,4},{1,5},{2,6},{3,7},{4,12},{5,13},{6,14},{7,15},{8,0},{9,1},{1... | collective-permute-start | bytes 49160 | tf_op jit(solution)/shard_map/ppermute | solution.py:23
  52.5 5.5 %collective-permute-start.28 = (f32[1,4,1024]{2,1,0:T(4,128)S(1)}, f32[1,4,1024]{2,1,0:T(4,128)S(1)}, u32[]{:S(2)}, u32[]{:S(2)}) collective-permute-start(f32[1,4,1024]{2,1,0:T(4,128)S(1)} %get-tuple-element.18), channel_id=1, source_target_pairs={{0,12},{1,13},{2,14},{3,15},{4,8},{5,9},{6,10},{7,11},{8,4},{9,5},... | collective-permute-start | bytes 49160 | tf_op jit(solution)/shard_map/ppermute | solution.py:23
  63.5 5.2 %collective-permute-start.30 = (bf16[4,8192]{1,0:T(4,128)(2,1)S(1)}, bf16[4,8192]{1,0:T(4,128)(2,1)S(1)}, u32[]{:S(2)}, u32[]{:S(2)}) collective-permute-start(bf16[4,8192]{1,0:T(4,128)(2,1)S(1)} %shard_map.84.refs_0_), channel_id=1, source_target_pairs={{0,4},{1,5},{2,6},{3,7},{4,12},{5,13},{6,14},{7,15},{8,0},{9,1},{1... | collective-permute-start | bytes 196616 | tf_op jit(solution)/shard_map/ppermute | solution.py:23
  65.5 6.2 %collective-permute-start.33 = (bf16[4,8192]{1,0:T(4,128)(2,1)S(1)}, bf16[4,8192]{1,0:T(4,128)(2,1)S(1)}, u32[]{:S(2)}, u32[]{:S(2)}) collective-permute-start(bf16[4,8192]{1,0:T(4,128)(2,1)S(1)} %shard_map.84.refs_0_), channel_id=1, source_target_pairs={{0,2},{1,3},{2,0},{3,1},{4,6},{5,7},{6,4},{7,5},{8,10},{9,11},{10,... | collective-permute-start | bytes 196616 | tf_op jit(solution)/shard_map/ppermute | solution.py:23
  68.8 4.9 %collective-permute-start.32 = (bf16[4,4096]{1,0:T(4,128)(2,1)S(1)}, bf16[4,4096]{1,0:T(4,128)(2,1)S(1)}, u32[]{:S(2)}, u32[]{:S(2)}) collective-permute-start(bf16[4,4096]{1,0:T(4,128)(2,1)S(1)} %slice.133), channel_id=1, source_target_pairs={{0,4},{1,5},{2,6},{3,7},{4,12},{5,13},{6,14},{7,15},{8,0},{9,1},{1... | collective-permute-start | bytes 98312 | tf_op jit(solution)/shard_map/ppermute | solution.py:23
  72.0 4.7 %collective-permute-start.39 = (bf16[4,8192]{1,0:T(4,128)(2,1)S(1)}, bf16[4,8192]{1,0:T(4,128)(2,1)S(1)}, u32[]{:S(2)}, u32[]{:S(2)}) collective-permute-start(bf16[4,8192]{1,0:T(4,128)(2,1)S(1)} %collective-permute-done.29.refs_1_), channel_id=1, source_target_pairs={{0,1},{1,0},{2,3},{3,2},{4,5},{5,4},{6,7},{7,6},{8,9},{9,8},{10,11... | collective-permute-start | bytes 196616 | tf_op jit(solution)/shard_map/ppermute | solution.py:23
  72.0 4.7 %collective-permute-start.40 = (bf16[4,8192]{1,0:T(4,128)(2,1)S(1)}, bf16[4,8192]{1,0:T(4,128)(2,1)S(1)}, u32[]{:S(2)}, u32[]{:S(2)}) collective-permute-start(bf16[4,8192]{1,0:T(4,128)(2,1)S(1)} %collective-permute-done.30.refs_2_), channel_id=1, source_target_pairs={{0,1},{1,0},{2,3},{3,2},{4,5},{5,4},{6,7},{7,6},{8,9},{9,8},{10,11... | collective-permute-start | bytes 196616 | tf_op jit(solution)/shard_map/ppermute | solution.py:23
  93.7 5.2 %collective-permute-start.50 = (bf16[4,4,1024]{2,1,0:T(4,128)(2,1)S(1)}, bf16[4,4,1024]{2,1,0:T(4,128)(2,1)S(1)}, u32[]{:S(2)}, u32[]{:S(2)}) collective-permute-start(bf16[4,4,1024]{2,1,0:T(4,128)(2,1)S(1)} %get-tuple-element.10), channel_id=1, source_target_pairs={{0,4},{1,5},{2,6},{3,7},{4,12},{5,13},{6,14},{7,15},{8,0},{9,1},{1... | collective-permute-start | bytes 98312 | tf_op jit(solution)/shard_map/ppermute | solution.py:23
  96.7 5.7 %collective-permute-start.52 = (bf16[4,4,1024]{2,1,0:T(4,128)(2,1)S(1)}, bf16[4,4,1024]{2,1,0:T(4,128)(2,1)S(1)}, u32[]{:S(2)}, u32[]{:S(2)}) collective-permute-start(bf16[4,4,1024]{2,1,0:T(4,128)(2,1)S(1)} %get-tuple-element.11), channel_id=1, source_target_pairs={{0,12},{1,13},{2,14},{3,15},{4,8},{5,9},{6,10},{7,11},{8,4},{9,5},... | collective-permute-start | bytes 98312 | tf_op jit(solution)/shard_map/ppermute | solution.py:23
  (33 other events, 158.8 us)
